TPU v7x, 1024 devices: a whole 4x8x16 slice. The times are simulated.
1024 devices in a mesh: dp: 16 (over y, x_hi), fsdp: 64 (over x_lo, z, core).
Axes of the slice: x: 4 (x_hi: 2, x_lo: 2; x = x_hi * 2 + x_lo), y: 8, z: 16, core: 2. Of those that a mesh axis runs over, the one named last changes fastest.
Arguments:
- attn_out: bfloat16 [18432, 4096], P('fsdp', 'dp'), may hold values from -6 to 6
- residual: bfloat16 [18432, 4096], P('fsdp', 'dp'), may hold values from -32 to 32
- out_proj: bfloat16 [4096, 4096], P('fsdp', 'dp'), may hold values from -0.09375 to 0.09375
- gain: float32 [4096], P('dp'), may hold values from 0.3 to 3
- positives: int32 [6144], P('fsdp'), may hold values from 0 to 191
Outputs:
- logits: float32 [6144, 192], P('fsdp')
- dlogits: float32 [6144, 192], P('fsdp')
- d_attn: bfloat16 [18432, 4096], P('fsdp', 'dp')
- d_resid: float32 [18432, 4096], P('fsdp', 'dp')
All inputs are finite; a program needn't handle non-finite values.
Results may differ from a plain program's by a relative error of at most 0.02.
Values may be sent and summed in bfloat16 or wider, within the bound.
A program may use at most 32 MiB of HBM per device.

v0:
```python
import jax
import jax.numpy as jnp
from jax import lax
from jax.sharding import PartitionSpec as P

QRY = 96


logit_scale = 20.0
loss_scale = 1024.0
highest = lax.Precision.HIGHEST


def inner_rows(left, right):
    return lax.dot_general(
        left, right, (((1,), (1,)), ((), ())), precision=highest, preferred_element_type=jnp.float32
    )


def inner_cols(left, right):
    return lax.dot_general(
        left, right, (((0,), (0,)), ((), ())), precision=highest, preferred_element_type=jnp.float32
    )


def shards(attn_out, residual, out_proj, gain, positives):
    features = lax.all_gather(attn_out, "dp", axis=1, tiled=True)
    panel = lax.all_gather(out_proj, "fsdp", axis=0, tiled=True)
    mixed = jnp.dot(features, panel, preferred_element_type=jnp.float32)
    scaled = (residual.astype(jnp.float32) + mixed) * gain[None, :]
    queries = scaled[:QRY]
    passages = scaled[QRY:]
    whole = lax.all_gather(scaled.astype(jnp.bfloat16), "dp", axis=1, tiled=True).astype(
        scaled.dtype
    )
    squares = jnp.sum(whole * whole, axis=1)
    dots = inner_rows(whole[:QRY], whole[QRY:])
    norms = jnp.sqrt(squares + 1e-06)
    query_norm = norms[:QRY]
    passage_norm = norms[QRY:]
    logits = logit_scale * dots / (query_norm[:, None] * passage_norm[None, :])
    shifted = jnp.exp(logits - logit_scale)
    probs = shifted / jnp.sum(shifted, axis=1, keepdims=True)
    target = (positives[:, None] == lax.broadcasted_iota(jnp.int32, probs.shape, 1)).astype(
        jnp.float32
    )
    dlogits = probs - target
    weighted = dlogits * logits
    unit_q = queries / query_norm[:, None]
    unit_p = passages / passage_norm[:, None]
    grad_q = (
        logit_scale * jnp.dot(dlogits, unit_p, precision=highest)
        - jnp.sum(weighted, axis=1)[:, None] * unit_q
    ) / query_norm[:, None]
    grad_p = (
        logit_scale * inner_cols(dlogits, unit_q) - jnp.sum(weighted, axis=0)[:, None] * unit_p
    ) / passage_norm[:, None]
    d_resid = loss_scale * gain[None, :] * jnp.concatenate([grad_q, grad_p], axis=0)
    d_mixed = d_resid.astype(jnp.bfloat16)
    term = lax.dot_general(
        d_mixed, panel, (((1,), (1,)), ((), ())), preferred_element_type=jnp.float32
    )
    d_attn = lax.psum_scatter(term.astype(jnp.bfloat16), "dp", scatter_dimension=1, tiled=True)
    return (logits, dlogits, d_attn, d_resid)


def solution(mesh):
    return jax.shard_map(
        shards,
        mesh=mesh,
        in_specs=(P("fsdp", "dp"), P("fsdp", "dp"), P("fsdp", "dp"), P("dp"), P("fsdp")),
        out_specs=(P("fsdp", None), P("fsdp", None), P("fsdp", "dp"), P("fsdp", "dp")),
        check_vma=False,
    )
```

profile of v0, /device:TPU:56, one launch (start us, length us, event | category | flops | bytes accessed | tf_op | source)
XLA Modules:
  0.0 589.8 jit_solution(4248402675387994394)
XLA Ops:
  7.2 0.0 all-gather.6.cloned.1.call-start
  7.2 0.7 all-gather.6.cloned.1.call-update
  7.9 0.0 all-gather.4.cloned.1.call-start
  7.9 0.7 all-gather.4.cloned.1.call-update
  8.6 0.0 copy-start.5
  8.7 0.0 all-gather.8.cloned.1.call-start
  8.7 135.0 %all-gather.6.cloned.1.call-done = bf16[4096,256]{1,0:T(8,128)(2,1)} async-done(((bf16[64,256]{1,0:T(8,128)(2,1)}), bf16[4096,256]{1,0:T(8,128)(2,1)}) %all-gather.6.cloned.1.call-update) | async-done | bytes 2097168 | tf_op jit(solution)/shard_map/all_gather | solution.py:28
  143.7 103.5 %all-gather.4.cloned.1.call-done = bf16[288,4096]{1,0:T(8,128)(2,1)} async-done(((bf16[288,256]{1,0:T(8,128)(2,1)}), bf16[288,4096]{1,0:T(8,128)(2,1)}) %all-gather.4.cloned.1.call-update) | async-done | bytes 2359312 | tf_op jit(solution)/shard_map/all_gather | solution.py:27
  247.3 3.7 fusion.16
  251.0 0.0 all-gather.8.cloned.1.call-update
  251.0 0.0 reduce-scatter.2.cloned.1.call-start
  251.1 0.0 copy-done.5
  251.1 101.7 %all-gather.8.cloned.1.call-done = bf16[288,4096]{1,0:T(8,128)(2,1)} async-done(((bf16[288,256]{1,0:T(8,128)(2,1)}), bf16[288,4096]{1,0:T(8,128)(2,1)}) %all-gather.8.cloned.1.call-update) | async-done | bytes 2359312 | tf_op jit(solution)/shard_map/all_gather | solution.py:33
  352.8 0.0 copy-start
  352.8 2.4 multiply_reduce_fusion
  355.1 0.0 copy-start.6
  355.2 0.1 slice.21
  355.2 0.0 copy-done
  355.2 0.7 fusion.15
  356.0 0.0 copy-start.3
  356.0 0.0 copy-start.2
  356.0 0.0 copy-done.6
  356.0 0.2 multiply_reduce_fusion.2
  356.2 0.0 copy-start.4
  356.2 0.3 fusion.12
  356.5 0.4 fusion.4
  357.0 0.7 copy-done.2
  357.6 0.0 copy-start.1
  357.7 2.2 convolution_convert_fusion
  359.9 0.0 copy-done.3
  359.9 0.0 copy-done.4
  359.9 0.0 copy-done.1
  359.9 0.0 reduce-scatter.2.cloned.1.call-update
  359.9 223.3 %reduce-scatter.2.cloned.1.call-done = bf16[288,256]{1,0:T(8,128)(2,1)} async-done(((bf16[288,4096]{1,0:T(8,128)(2,1)}), bf16[288,256]{1,0:T(8,128)(2,1)}) %reduce-scatter.2.cloned.1.call-update) | async-done | bytes 147472 | tf_op jit(solution)/shard_map/reduce_scatter | solution.py:63
  (4 shorter events, 0.0 us)
Async XLA Ops:
  7.2 136.6 %all-gather.6.cloned.1.call-start = ((), (), s32[]{:S(2)}) async-start(), calls=%async_computation.2 | async-start | bytes 2129920 | tf_op jit(solution)/shard_map/all_gather | solution.py:28
  7.9 239.4 %all-gather.4.cloned.1.call-start = ((), (), s32[]{:S(2)}) async-start(), calls=%async_computation.1 | async-start | bytes 2506752 | tf_op jit(solution)/shard_map/all_gather | solution.py:27
  8.6 242.4 %copy-start.5 = (f32[256]{0:T(256)S(1)}, f32[256]{0:T(256)}, u32[]{:S(2)}) copy-start(f32[256]{0:T(256)} %param.8) | copy-start | bytes 3076
  8.7 344.1 %all-gather.8.cloned.1.call-start = ((), (), s32[]{:S(2)}) async-start(), calls=%async_computation.3 | async-start | bytes 2506752 | tf_op jit(solution)/shard_map/all_gather | solution.py:33
  251.0 332.2 %reduce-scatter.2.cloned.1.call-start = ((), (), s32[]{:S(2)}) async-start(), calls=%async_computation.4 | async-start | bytes 2506752 | tf_op jit(solution)/shard_map/reduce_scatter | solution.py:63
  352.8 2.5 copy-start
  355.1 0.9 copy-start.6
  356.0 3.9 copy-start.3
  356.0 1.7 copy-start.2
  356.2 3.7 copy-start.4
  357.6 2.2 copy-start.1
Sparse Core Ops, SparseCore 0:
  10.7 132.9 all-gather.5
  148.0 99.2 all-gather.3
  252.1 100.6 all-gather.7
  360.0 223.1 reduce-scatter.1
where the time goes:
time: 591 us; the launch traced here: 590 us
  waiting for transfers between devices  565 us (96%)
  between operations  13.9 us (2%)
  matrix products  7.42 us (1%)
    reduce_scatter x1, waiting for transfers between devices, shards(): lax.psum_scatter(term.astype(jnp.bfloat16), 'dp', scatter_dimension=1, ti...  223 us
    all_gather x1, waiting for transfers between devices, shards(): panel = lax.all_gather(out_proj, 'fsdp', axis=0, tiled=True)  135 us
    all_gather x1, waiting for transfers between devices, shards(): features = lax.all_gather(attn_out, 'dp', axis=1, tiled=True)  104 us
    all_gather x1, waiting for transfers between devices, shards(): lax.all_gather(scaled.astype(jnp.bfloat16), 'dp', axis=1, tiled=True)  102 us
  transfers between devices with their start and end apart: 4, of which 4 were waited for; matrix products, arithmetic and copies ran while one was open for 0% of the time, Pallas kernels for 0%

commit v1 on v0

v1 whole, which is shorter than its diff:
```python
import jax
import jax.numpy as jnp
from jax import lax
from jax.experimental import pallas as pl
from jax.experimental.pallas import tpu as pltpu
from jax.sharding import PartitionSpec as P

QRY = 96
PSG = 192
GROUP = 288
W = 256
NY, NZ = 8, 16
ROWS_X = 128
ROWS_Y = GROUP - ROWS_X
SLICES = QRY // 8

logit_scale = 20.0
loss_scale = 1024.0
highest = lax.Precision.HIGHEST
f32 = jnp.float32
bf16 = jnp.bfloat16
MESH = pl.DeviceIdType.MESH


def device(y, h, l, z, k):
    return (y * 2 + h, l * 32 + z * 2 + k)


def dot_t(left, right, precision=None):
    return lax.dot_general(
        left, right, (((1,), (1,)), ((), ())), precision=precision, preferred_element_type=f32
    )


def remote(src, dst, send, recv, target):
    return pltpu.make_async_remote_copy(
        src_ref=src, dst_ref=dst, send_sem=send, recv_sem=recv, device_id=target, device_id_type=MESH
    )


ROWS = {"a": (0, ROWS_X), "p": (0, ROWS_X), "b": (ROWS_X, ROWS_Y)}


def rows_of(kind, hop, way):
    start, size = ROWS[kind]
    if hop < 3:
        return start, size
    return start + way * (size // 2), size // 2


def main_kernel(
    attn_hbm, resid_hbm, weight_hbm, gain,
    t_out, scaled_out, z_out,
    g, wp, t, so, sp, ro, rp, xs, xr, ps, pr, zpart, zin, zsum,
    ag_s, ag_r, ax_s, ax_r, bx_s, bx_r, wl_s, wl_r, wz_s, wz_r, wk_s, wk_r,
    rs_s, rs_r, rx_s, rx_r, rp_s, rp_r, z1_s, z1_r, z2_s, z2_r,
    resid, in_sem,
):
    c = lax.axis_index("dp")
    f = lax.axis_index("fsdp")
    y, h = c // 2, c % 2
    l, z, k = f // 32, (f // 2) % 16, f % 2
    across = device(y, 1 - h, l, z, k)
    beside = device(y, h, 1 - l, z, k)
    sibling = device(y, h, l, z, 1 - k)
    along = (device((y + 1) % NY, h, l, z, k), device((y + NY - 1) % NY, h, l, z, k))
    z_near = (device(y, h, l, (z + 1) % NZ, k), device(y, h, l, (z + NZ - 1) % NZ, k))
    z_far = (device(y, h, l, (z + 2) % NZ, k), device(y, h, l, (z + NZ - 2) % NZ, k))
    peers = [((c + r) % 16, f) for r in range(1, 16)]

    barrier = pltpu.get_barrier_semaphore()
    everyone = peers + [beside, sibling, *z_near, *z_far]
    for target in everyone:
        pl.semaphore_signal(barrier, inc=1, device_id=target, device_id_type=MESH)
    load_a = pltpu.make_async_copy(attn_hbm, g.at[c], in_sem.at[0])
    load_w = pltpu.make_async_copy(weight_hbm, wp.at[l, z, k], in_sem.at[1])
    load_r = pltpu.make_async_copy(resid_hbm, resid, in_sem.at[2])
    load_a.start()
    load_w.start()
    load_r.start()
    load_a.wait()
    load_w.wait()
    load_r.wait()
    pl.semaphore_wait(barrier, len(everyone))

    def slot(step, other=0):
        return ((y + step + NY) % NY) * 2 + (1 - h if other else h)

    KINDS = ("a", "b", "p")

    def ag(kind, way, hop):
        start, size = rows_of(kind, hop, way)
        block = g.at[slot(-hop if way == 0 else hop, kind == "p"), pl.ds(start, size)]
        i = KINDS.index(kind)
        return remote(block, block, ag_s.at[i, way, hop], ag_r.at[i, way, hop], along[way])

    def ag_recv(kind, way, hop):
        start, size = rows_of(kind, hop, way)
        block = g.at[slot(-hop - 1 if way == 0 else hop + 1, kind == "p"), pl.ds(start, size)]
        i = KINDS.index(kind)
        return remote(block, block, ag_s.at[i, way, hop], ag_r.at[i, way, hop], along[way])

    def ax(other=0):
        block = g.at[slot(0, other), pl.ds(0, ROWS_X)]
        return remote(block, block, ax_s, ax_r, across)

    steps = [(0, ROWS_X, ROWS_Y)]
    for d in (1, 2, 3):
        steps += [(-d, ROWS_X, ROWS_Y), (d, ROWS_X, ROWS_Y)]
    steps += [(4, ROWS_X, ROWS_Y // 2), (4, ROWS_X + ROWS_Y // 2, ROWS_Y // 2)]

    def bx(i, other=0):
        step, start, size = steps[i]
        block = g.at[slot(step, other), pl.ds(start, size)]
        return remote(block, block, bx_s.at[i], bx_r.at[i], across)

    def wz(u, way, dist):
        hop = 2 if dist % 2 == 0 else 1
        back = dist - hop
        zz = (z - back + NZ) % NZ if way == 0 else (z + back) % NZ
        block = wp.at[1 - l if u else l, zz, k]
        target = (z_far if hop == 2 else z_near)[way]
        return remote(block, block, wz_s.at[u, way, dist - 1], wz_r.at[u, way, dist - 1], target)

    def wz_recv(u, way, dist):
        zz = (z - dist + NZ) % NZ if way == 0 else (z + dist) % NZ
        block = wp.at[1 - l if u else l, zz, k]
        return remote(block, block, wz_s.at[u, way, dist - 1], wz_r.at[u, way, dist - 1], z_near[way])

    def reach(way):
        return 8 if way == 0 else 7

    def wl(u=0):
        block = wp.at[1 - l if u else l, z, k]
        return remote(block, block, wl_s, wl_r, beside)

    def wk(way, dist, core):
        zz = (z - dist + NZ) % NZ if way == 0 else (z + dist) % NZ
        block = wp.at[:, zz, core]
        return remote(block, block, wk_s.at[way, dist], wk_r.at[way, dist], sibling)

    def wz_start(u, way, stage):
        for dist in (2 * stage + 2, 2 * stage + 1):
            if dist <= reach(way):
                wz(u, way, dist).start()

    ax().start()
    wl().start()
    for way in (0, 1):
        ag("a", way, 0).start()
        wz_start(0, way, 0)
        ag("b", way, 0).start()
    bx(0).start()
    wl(1).wait_recv()
    for way in (0, 1):
        wz_start(1, way, 0)
    wk(0, 0, k).start()
    ax(1).wait_recv()
    for way in (0, 1):
        ag("p", way, 0).start()
    for hop in range(4):
        for kind in KINDS:
            for way in (0, 1):
                ag_recv(kind, way, hop).wait_recv()
                if hop < 3:
                    ag(kind, way, hop + 1).start()
                if kind == "b":
                    bx(1 + 2 * hop + way).start()
            if kind == "a":
                u = 0
            elif kind == "p":
                u = 1
            else:
                continue
            for way in (0, 1):
                if 2 * hop + 2 <= reach(way):
                    wz_recv(u, way, 2 * hop + 2).wait_recv()
                    if hop < 3:
                        wz_start(u, way, hop + 1)
        for way in (0, 1):
            for dist in (2 * hop + 1, 2 * hop + 2):
                if dist <= reach(way):
                    if dist % 2:
                        wz_recv(0, way, dist).wait_recv()
                        wz_recv(1, way, dist).wait_recv()
                    wk(way, dist, k).start()
    for i in range(9):
        bx(i, 1).wait_recv()
    wk(0, 0, 1 - k).wait_recv()
    for way in (0, 1):
        for dist in range(1, reach(way) + 1):
            wk(way, dist, 1 - k).wait_recv()

    def panel(index):
        return wp[index // 8, pl.ds(2 * (index % 8), 2)].reshape(W, W)

    total = jnp.dot(g[0], panel(0), preferred_element_type=f32)
    for j in range(1, 16):
        total = total + jnp.dot(g[j], panel(j), preferred_element_type=f32)
    scaled = (resid[...].astype(f32) + total) * gain[...]
    scaled_out[...] = scaled

    queries, passages = scaled[:QRY], scaled[QRY:]
    zpart[:, :PSG] = dot_t(queries, passages, highest)
    squares = jnp.sum(scaled * scaled, axis=1, keepdims=True)
    lane = lax.broadcasted_iota(jnp.int32, (QRY, W - PSG), 1)
    zpart[:, PSG:] = jnp.where(
        lane == 0, squares[:QRY], jnp.where(lane == 1, squares[QRY : 2 * QRY], squares[2 * QRY :])
    )

    def z1(r):
        to = (c + r) % 16
        return to, remote(
            zpart.at[pl.ds(pl.multiple_of(8 * to, 8), 8)], zin.at[c], z1_s.at[r], z1_r.at[r], (to, f)
        )

    for r in range(1, 16):
        to = (c + r) % 16

        @pl.when(to < SLICES)
        def _():
            z1(r)[1].start()

    u = (scaled * gain[...]).astype(bf16)

    def term(step, other):
        index = slot(step, other)
        t[index] = dot_t(u, panel(index))

    def rx(i):
        return remote(xs.at[i], xr.at[i], rx_s.at[i], rx_r.at[i], across)

    order = (4, 3, -3, 2, -2, 1, -1, 0)

    def x_send(step):
        i = order.index(step)
        xs[i] = t[slot(step, 1), ROWS_X:].astype(bf16)
        rx(i).start()

    def rs(kind, way, stage):
        start, size = rows_of(kind, 3 - stage, way)
        if kind == "p":
            src, dst = sp.at[way, stage, pl.ds(start, size)], rp.at[way, stage, pl.ds(start, size)]
        else:
            src, dst = so.at[way, stage, pl.ds(start, size)], ro.at[way, stage, pl.ds(start, size)]
        i = KINDS.index(kind)
        return remote(src, dst, rs_s.at[i, way, stage], rs_r.at[i, way, stage], along[way])

    def own(kind, step, start, size):
        value = t[slot(step, kind == "p"), pl.ds(start, size)]
        if kind == "b":
            value = value + xr[order.index(step), pl.ds(start - ROWS_X, size)].astype(f32)
        return value

    def rs_send(kind, way, stage):
        dist = 4 - stage
        step = 4 if dist == 4 else (dist if way == 0 else -dist)
        out = sp if kind == "p" else so
        start, size = rows_of(kind, 3 - stage, way)
        got = rp if kind == "p" else ro
        if stage == 0:
            out[way, 0, pl.ds(start, size)] = own(kind, step, start, size).astype(bf16)
        elif stage == 1:
            rs(kind, way, 0).wait_recv()
            first, part = rows_of(kind, 3, way)
            rest, _ = rows_of(kind, 3, 1 - way)
            out[way, 1, pl.ds(first, part)] = (
                own(kind, step, first, part) + got[way, 0, pl.ds(first, part)].astype(f32)
            ).astype(bf16)
            out[way, 1, pl.ds(rest, part)] = own(kind, step, rest, part).astype(bf16)
        else:
            rs(kind, way, stage - 1).wait_recv()
            out[way, stage, pl.ds(start, size)] = (
                own(kind, step, start, size) + got[way, stage - 1, pl.ds(start, size)].astype(f32)
            ).astype(bf16)
        rs(kind, way, stage).start()

    for step in order:
        term(step, 1)
        x_send(step)
        term(step, 0)
        if step == 4:
            for kind in ("p", "a"):
                for way in (0, 1):
                    rs_send(kind, way, 0)
    rx(0).wait_recv()
    for way in (0, 1):
        rs_send("b", way, 0)

    def z2(r):
        to = (c + r) % 16
        mine = zsum.at[pl.ds(pl.multiple_of(8 * c, 8), 8)]
        return remote(mine, mine, z2_s.at[r], z2_r.at[r], (to, f))

    for stage in (1, 2, 3):
        for kind in ("p", "a", "b"):
            for way in (0, 1):
                if kind == "b":
                    dist = 4 - stage
                    rx(order.index(dist if way == 0 else -dist)).wait_recv()
                rs_send(kind, way, stage)
        if stage == 1:

            @pl.when(c < SLICES)
            def _():
                for r in range(1, 16):
                    theirs = zin.at[(c + 16 - r) % 16]
                    remote(theirs, theirs, z1_s.at[r], z1_r.at[r], ((c + r) % 16, f)).wait_recv()
                zin[c] = zpart[pl.ds(pl.multiple_of(8 * c, 8), 8)]
                acc = zin[0]
                for j in range(1, 16):
                    acc = acc + zin[j]
                zsum[pl.ds(pl.multiple_of(8 * c, 8), 8)] = acc
                for r in range(1, 16):
                    z2(r).start()

    def landed(kind):
        start, size = ROWS[kind]
        got = rp if kind == "p" else ro
        for way in (0, 1):
            rs(kind, way, 3).wait_recv()
        return (
            own(kind, 0, start, size)
            + got[0, 3, pl.ds(start, size)].astype(f32)
            + got[1, 3, pl.ds(start, size)].astype(f32)
        )

    last = remote(ps, pr, rp_s, rp_r, across)
    ps[...] = landed("p").astype(bf16)
    last.start()
    a_sum = landed("a")
    rx(order.index(0)).wait_recv()
    t_out[ROWS_X:] = landed("b")
    last.wait_recv()
    t_out[:ROWS_X] = a_sum + pr[...].astype(f32)

    for r in range(1, 16):
        by = (c + 16 - r) % 16

        @pl.when(by < SLICES)
        def _():
            theirs = zsum.at[pl.ds(pl.multiple_of(8 * by, 8), 8)]
            remote(theirs, theirs, z2_s.at[r], z2_r.at[r], (by, f)).wait_recv()

    z_out[...] = zsum[...]

    ax().wait_send()
    wl().wait_send()
    for i in range(9):
        bx(i).wait_send()
    for way in (0, 1):
        for hop in range(4):
            for kind in KINDS:
                ag(kind, way, hop).wait_send()
                rs(kind, way, hop).wait_send()
        for dist in range(1, reach(way) + 1):
            wz(0, way, dist).wait_send()
            wz(1, way, dist).wait_send()
            wk(way, dist, k).wait_send()
    wk(0, 0, k).wait_send()
    for i in range(8):
        rx(i).wait_send()
    last.wait_send()
    for r in range(1, 16):

        @pl.when((c + r) % 16 < SLICES)
        def _():
            z1(r)[1].wait_send()

    @pl.when(c < SLICES)
    def _():
        for r in range(1, 16):
            z2(r).wait_send()


def tail_kernel(total, scaled, inner, gain, positives, logits_out, dlogits_out, d_attn, d_resid):
    eye = lax.broadcasted_iota(jnp.int32, (QRY, QRY), 0) == lax.broadcasted_iota(
        jnp.int32, (QRY, QRY), 1
    )

    def as_row(column):
        return jnp.sum(jnp.where(eye, column, 0.0), axis=0, keepdims=True)

    norm_q = jnp.sqrt(inner[:, PSG : PSG + 1] + 1e-06)
    norm_p1 = jnp.sqrt(inner[:, PSG + 1 : PSG + 2] + 1e-06)
    norm_p2 = jnp.sqrt(inner[:, PSG + 2 : PSG + 3] + 1e-06)
    norm_p = jnp.concatenate([norm_p1, norm_p2], axis=0)
    row_p = jnp.concatenate([as_row(norm_p1), as_row(norm_p2)], axis=1)
    logits = logit_scale * inner[:, :PSG] / (norm_q * row_p)
    shifted = jnp.exp(logits - logit_scale)
    probs = shifted / jnp.sum(shifted, axis=1, keepdims=True)
    wanted = jnp.sum(jnp.where(eye, positives[...], 0), axis=1, keepdims=True)
    target = (wanted == lax.broadcasted_iota(jnp.int32, (QRY, PSG), 1)).astype(f32)
    dlogits = probs - target
    logits_out[...] = logits
    dlogits_out[...] = dlogits
    weighted = dlogits * logits
    sum_q = jnp.sum(weighted, axis=1, keepdims=True)
    sum_p_row = jnp.sum(weighted, axis=0, keepdims=True)
    sum_p = jnp.concatenate(
        [
            jnp.sum(jnp.where(eye, sum_p_row[:, :QRY], 0.0), axis=1, keepdims=True),
            jnp.sum(jnp.where(eye, sum_p_row[:, QRY:], 0.0), axis=1, keepdims=True),
        ],
        axis=0,
    )

    def through(rows):
        unit_q = rows[:QRY] / norm_q
        unit_p = rows[QRY:] / norm_p
        grad_q = (
            logit_scale
            * jnp.dot(dlogits, unit_p, precision=highest, preferred_element_type=f32)
            - sum_q * unit_q
        ) / norm_q
        grad_p = (
            logit_scale
            * lax.dot_general(
                dlogits, unit_q, (((0,), (0,)), ((), ())), precision=highest,
                preferred_element_type=f32,
            )
            - sum_p * unit_p
        ) / norm_p
        return grad_q, grad_p

    grad_q, grad_p = through(scaled[...])
    scale = loss_scale * gain[...]
    d_resid[:QRY] = scale * grad_q
    d_resid[QRY:] = scale * grad_p
    grad_q, grad_p = through(total[...])
    d_attn[:QRY] = (loss_scale * grad_q).astype(bf16)
    d_attn[QRY:] = (loss_scale * grad_p).astype(bf16)


def shards(attn_out, residual, out_proj, gain, positives):
    vmem = pl.BlockSpec(memory_space=pltpu.VMEM)
    hbm = pl.BlockSpec(memory_space=pltpu.HBM)
    dma = pltpu.SemaphoreType.DMA
    gain = gain.reshape(1, W)
    total, scaled, inner = pl.pallas_call(
        main_kernel,
        out_shape=(
            jax.ShapeDtypeStruct((GROUP, W), f32),
            jax.ShapeDtypeStruct((GROUP, W), f32),
            jax.ShapeDtypeStruct((QRY, W), f32),
        ),
        in_specs=[hbm, hbm, hbm, vmem],
        out_specs=[vmem] * 3,
        scratch_shapes=[
            pltpu.VMEM((16, GROUP, W), bf16),
            pltpu.VMEM((2, NZ, 2, 64, W), bf16),
            pltpu.VMEM((16, GROUP, W), f32),
            pltpu.VMEM((2, 4, GROUP, W), bf16),
            pltpu.VMEM((2, 4, ROWS_X, W), bf16),
            pltpu.VMEM((2, 4, GROUP, W), bf16),
            pltpu.VMEM((2, 4, ROWS_X, W), bf16),
            pltpu.VMEM((8, ROWS_Y, W), bf16),
            pltpu.VMEM((8, ROWS_Y, W), bf16),
            pltpu.VMEM((ROWS_X, W), bf16),
            pltpu.VMEM((ROWS_X, W), bf16),
            pltpu.VMEM((QRY, W), f32),
            pltpu.VMEM((16, 8, W), f32),
            pltpu.VMEM((QRY, W), f32),
            dma((3, 2, 4)), dma((3, 2, 4)),
            dma, dma,
            dma((9,)), dma((9,)),
            dma, dma,
            dma((2, 2, 8)), dma((2, 2, 8)),
            dma((2, 9)), dma((2, 9)),
            dma((3, 2, 4)), dma((3, 2, 4)),
            dma((8,)), dma((8,)),
            dma, dma,
            dma((16,)), dma((16,)),
            dma((16,)), dma((16,)),
            pltpu.VMEM((GROUP, W), bf16),
            dma((3,)),
        ],
        compiler_params=pltpu.CompilerParams(
            collective_id=0, has_side_effects=True, vmem_limit_bytes=40 * 2**20
        ),
    )(attn_out, residual, out_proj, gain)
    return pl.pallas_call(
        tail_kernel,
        out_shape=(
            jax.ShapeDtypeStruct((QRY, PSG), f32),
            jax.ShapeDtypeStruct((QRY, PSG), f32),
            jax.ShapeDtypeStruct((GROUP, W), bf16),
            jax.ShapeDtypeStruct((GROUP, W), f32),
        ),
        in_specs=[vmem] * 5,
        out_specs=[vmem] * 4,
        compiler_params=pltpu.CompilerParams(vmem_limit_bytes=32 * 2**20),
    )(total, scaled, inner, gain, positives.reshape(1, QRY))


def solution(mesh):
    return jax.shard_map(
        shards,
        mesh=mesh,
        in_specs=(P("fsdp", "dp"), P("fsdp", "dp"), P("fsdp", "dp"), P("dp"), P("fsdp")),
        out_specs=(P("fsdp", None), P("fsdp", None), P("fsdp", "dp"), P("fsdp", "dp")),
        check_vma=False,
    )
```

time: 591 us -> 83.8 us (0.14)
  waiting for transfers between devices: 565 us -> 0 us
  Pallas kernels: 0 us -> 79 us
  between operations: 13.9 us -> 0.66 us
  matrix products: 7.42 us -> 0 us
    all_gather x3 -> x0, waiting for transfers between devices: 340 us -> none  [the longest x1 135 us: shards(): panel = lax.all_gather(out_proj, 'fsdp', axis=0, tiled=True)]
    reduce_scatter x1 -> x0, waiting for transfers between devices: 223 us -> none  [shards(): lax.psum_scatter(term.astype(jnp.bfloat16), 'dp', scatter_dimension=1, ti...]
    pallas_call x0 -> x2, Pallas kernels: none -> 79 us  [the longest x1 77.3 us: shards(): pl.pallas_call(main_kernel, out_shape=(jax.ShapeDtypeStruct((GROUP, W), f...]
    dot_general x5 -> x0, matrix products: 7.42 us -> none  [the longest x1 3.74 us: shards(): mixed = jnp.dot(features, panel, preferred_element_type=jnp.float32)]
  transfers between devices with their start and end apart: 4 -> 0, of which waited for: 4 -> 0; matrix products, arithmetic and copies ran while one was open for 0% -> 0% of each run, Pallas kernels for 0% -> 0%
where the time goes in v1:
time: 83.8 us; the launch traced here: 83.6 us
  Pallas kernels  79 us (94%)
  local copies, waits for them, and re-layouts  3.9 us (5%)
    pallas_call x1, Pallas kernels, shards(): pl.pallas_call(main_kernel, out_shape=(jax.ShapeDtypeStruct((GROUP, W), f...  77.3 us
    unnamed x10, local copies, waits for them, and re-layouts  3.9 us
    pallas_call x1, Pallas kernels, shards(): pl.pallas_call(tail_kernel, out_shape=(jax.ShapeDtypeStruct((QRY, PSG), f...  1.7 us

profile of v1, /device:TPU:56, one launch (start us, length us, event | category | flops | bytes accessed | tf_op | source)
XLA Modules:
  0.0 83.6 jit_solution(4818319964979073586)
XLA Ops:
  0.6 0.0 copy-start.3
  0.6 0.7 copy-done.3
  1.3 0.0 copy-start
  1.3 0.9 %copy-done = bf16[288,256]{1,0:T(8,128)(2,1)S(1)} copy-done((bf16[288,256]{1,0:T(8,128)(2,1)S(1)}, bf16[288,256]{1,0:T(8,128)(2,1)}, u32[]{:S(2)}) %copy-start) | copy-done | bytes 147480
  2.2 0.0 copy-start.1
  2.2 0.9 %copy-done.1 = bf16[288,256]{1,0:T(8,128)(2,1)S(1)} copy-done((bf16[288,256]{1,0:T(8,128)(2,1)S(1)}, bf16[288,256]{1,0:T(8,128)(2,1)}, u32[]{:S(2)}) %copy-start.1) | copy-done | bytes 147480
  3.1 0.0 copy-start.2
  3.1 0.8 copy-done.2
  3.9 77.3 %shard_map.84 = (f32[288,256]{1,0:T(8,128)S(1)}, f32[288,256]{1,0:T(8,128)S(1)}, f32[96,256]{1,0:T(8,128)S(1)}) custom-call(bf16[288,256]{1,0:T(8,128)(2,1)S(1)} %copy-done, bf16[288,256]{1,0:T(8,128)(2,1)S(1)} %copy-done.1, bf16[64,256]{1,0:T(8,128)(2,1)S(1)} %copy-done.2, f32[1,256]{1,0:T(1,128)S(1)} %bitcast.2), custom_call_target="tpu_custom_call" | custom-call | tf_op jit(solution)/shard_map/pallas_call | solution.py:440
  81.2 0.0 copy-start.4
  81.2 0.6 copy-done.4
  81.9 1.7 %shard_map.85 = (f32[96,192]{1,0:T(8,128)}, f32[96,192]{1,0:T(8,128)}, bf16[288,256]{1,0:T(8,128)(2,1)}, f32[288,256]{1,0:T(8,128)}) custom-call(f32[288,256]{1,0:T(8,128)S(1)} %get-tuple-element.7.total, f32[288,256]{1,0:T(8,128)S(1)} %get-tuple-element.8.scaled, f32[96,256]{1,0:T(8,128)S(1)} %get-tuple-element.9.inner, f32[1,256]{1,0:T(1,128)S(1)} %bitcast.3, ...), custom_call_target="tpu_custom_call" | custom-call | tf_op jit(solution)/shard_map/pallas_call | solution.py:482
Async XLA Ops:
  0.6 0.7 copy-start.3
  1.3 0.9 %copy-start = (bf16[288,256]{1,0:T(8,128)(2,1)S(1)}, bf16[288,256]{1,0:T(8,128)(2,1)}, u32[]{:S(2)}) copy-start(bf16[288,256]{1,0:T(8,128)(2,1)} %attn_hbm.1) | copy-start | bytes 442372
  2.2 0.9 %copy-start.1 = (bf16[288,256]{1,0:T(8,128)(2,1)S(1)}, bf16[288,256]{1,0:T(8,128)(2,1)}, u32[]{:S(2)}) copy-start(bf16[288,256]{1,0:T(8,128)(2,1)} %resid_hbm.1) | copy-start | bytes 442372
  3.1 0.8 copy-start.2
  81.2 0.7 copy-start.4

commit v2 on v1

--- a/solution.py
+++ b/solution.py
@@ -211,7 +211,7 @@
     def z1(r):
         to = (c + r) % 16
         return to, remote(
-            zpart.at[pl.ds(pl.multiple_of(8 * to, 8), 8)], zin.at[c], z1_s.at[r], z1_r.at[r], (to, f)
+            zpart.at[pl.ds(pl.multiple_of(8 * to, 8), 8)], zin.at[c], z1_s, z1_r, (to, f)
         )
 
     for r in range(1, 16):
@@ -275,44 +275,57 @@
             ).astype(bf16)
         rs(kind, way, stage).start()
 
-    for step in order:
+    term(4, 1)
+    x_send(4)
+    for way in (0, 1):
+        rs_send("p", way, 0)
+    term(4, 0)
+    for way in (0, 1):
+        rs_send("a", way, 0)
+    for step in order[1:]:
         term(step, 1)
-        x_send(step)
+        if step in (3, -3):
+            x_send(step)
         term(step, 0)
-        if step == 4:
-            for kind in ("p", "a"):
-                for way in (0, 1):
-                    rs_send(kind, way, 0)
-    rx(0).wait_recv()
-    for way in (0, 1):
-        rs_send("b", way, 0)
 
     def z2(r):
         to = (c + r) % 16
         mine = zsum.at[pl.ds(pl.multiple_of(8 * c, 8), 8)]
-        return remote(mine, mine, z2_s.at[r], z2_r.at[r], (to, f))
-
-    for stage in (1, 2, 3):
-        for kind in ("p", "a", "b"):
-            for way in (0, 1):
-                if kind == "b":
-                    dist = 4 - stage
-                    rx(order.index(dist if way == 0 else -dist)).wait_recv()
-                rs_send(kind, way, stage)
+        return remote(mine, mine, z2_s, z2_r, (to, f))
+
+    def b_send(stage):
+        dist = 4 - stage
+        for way in (0, 1):
+            if stage > 0:
+                rx(order.index(dist if way == 0 else -dist)).wait_recv()
+            elif way == 0:
+                rx(0).wait_recv()
+            rs_send("b", way, stage)
+
+    def reduce_slice():
+        @pl.when(c < SLICES)
+        def _():
+            theirs = zin.at[pl.ds(0, 15)]
+            remote(theirs, theirs, z1_s, z1_r, peers[0]).wait_recv()
+            zin[c] = zpart[pl.ds(pl.multiple_of(8 * c, 8), 8)]
+            acc = zin[0]
+            for j in range(1, 16):
+                acc = acc + zin[j]
+            zsum[pl.ds(pl.multiple_of(8 * c, 8), 8)] = acc
+            for r in range(1, 16):
+                z2(r).start()
+
+    for stage, sends in ((1, (2, -2)), (2, (1, -1)), (3, (0,))):
+        for way in (0, 1):
+            rs_send("p", way, stage)
+        b_send(stage - 1)
+        for step in sends:
+            x_send(step)
+        for way in (0, 1):
+            rs_send("a", way, stage)
         if stage == 1:
-
-            @pl.when(c < SLICES)
-            def _():
-                for r in range(1, 16):
-                    theirs = zin.at[(c + 16 - r) % 16]
-                    remote(theirs, theirs, z1_s.at[r], z1_r.at[r], ((c + r) % 16, f)).wait_recv()
-                zin[c] = zpart[pl.ds(pl.multiple_of(8 * c, 8), 8)]
-                acc = zin[0]
-                for j in range(1, 16):
-                    acc = acc + zin[j]
-                zsum[pl.ds(pl.multiple_of(8 * c, 8), 8)] = acc
-                for r in range(1, 16):
-                    z2(r).start()
+            reduce_slice()
+    b_send(3)
 
     def landed(kind):
         start, size = ROWS[kind]
@@ -334,13 +347,17 @@
     last.wait_recv()
     t_out[:ROWS_X] = a_sum + pr[...].astype(f32)
 
-    for r in range(1, 16):
-        by = (c + 16 - r) % 16
-
-        @pl.when(by < SLICES)
-        def _():
-            theirs = zsum.at[pl.ds(pl.multiple_of(8 * by, 8), 8)]
-            remote(theirs, theirs, z2_s.at[r], z2_r.at[r], (by, f)).wait_recv()
+    def slices(ref, count, send, recv):
+        part = ref.at[pl.ds(0, 8 * count)]
+        return remote(part, part, send, recv, peers[0])
+
+    @pl.when(c < SLICES)
+    def _():
+        slices(zsum, SLICES - 1, z2_s, z2_r).wait_recv()
+
+    @pl.when(c >= SLICES)
+    def _():
+        slices(zsum, SLICES, z2_s, z2_r).wait_recv()
 
     z_out[...] = zsum[...]
 
@@ -361,16 +378,15 @@
     for i in range(8):
         rx(i).wait_send()
     last.wait_send()
-    for r in range(1, 16):
-
-        @pl.when((c + r) % 16 < SLICES)
-        def _():
-            z1(r)[1].wait_send()
-
     @pl.when(c < SLICES)
     def _():
-        for r in range(1, 16):
-            z2(r).wait_send()
+        slices(zpart, SLICES - 1, z1_s, z1_r).wait_send()
+        theirs = zin.at[pl.ds(0, 15)]
+        remote(theirs, theirs, z2_s, z2_r, peers[0]).wait_send()
+
+    @pl.when(c >= SLICES)
+    def _():
+        slices(zpart, SLICES, z1_s, z1_r).wait_send()
 
 
 def tail_kernel(total, scaled, inner, gain, positives, logits_out, dlogits_out, d_attn, d_resid):
@@ -470,8 +486,8 @@
             dma((3, 2, 4)), dma((3, 2, 4)),
             dma((8,)), dma((8,)),
             dma, dma,
-            dma((16,)), dma((16,)),
-            dma((16,)), dma((16,)),
+            dma, dma,
+            dma, dma,
             pltpu.VMEM((GROUP, W), bf16),
             dma((3,)),
         ],

time: 83.8 us -> 82.7 us (0.987)
  Pallas kernels: 79 us -> 77.7 us
    pallas_call x1, Pallas kernels: 77.3 us -> 76 us  [shards(): pl.pallas_call(main_kernel, out_shape=(jax.ShapeDtypeStruct((GROUP, W), f...]
where the time goes in v2:
time: 82.7 us; the launch traced here: 82.2 us
  Pallas kernels  77.7 us (94%)
  local copies, waits for them, and re-layouts  3.9 us (5%)
    pallas_call x1, Pallas kernels, shards(): pl.pallas_call(main_kernel, out_shape=(jax.ShapeDtypeStruct((GROUP, W), f...  76 us
    unnamed x10, local copies, waits for them, and re-layouts  3.9 us
    pallas_call x1, Pallas kernels, shards(): pl.pallas_call(tail_kernel, out_shape=(jax.ShapeDtypeStruct((QRY, PSG), f...  1.7 us

profile of v2, /device:TPU:56, one launch (start us, length us, event | category | flops | bytes accessed | tf_op | source)
XLA Modules:
  0.0 82.2 jit_solution(5240375334844710687)
XLA Ops:
  0.6 0.0 copy-start.3
  0.6 0.7 copy-done.3
  1.3 0.0 copy-start
  1.3 0.9 %copy-done = bf16[288,256]{1,0:T(8,128)(2,1)S(1)} copy-done((bf16[288,256]{1,0:T(8,128)(2,1)S(1)}, bf16[288,256]{1,0:T(8,128)(2,1)}, u32[]{:S(2)}) %copy-start) | copy-done | bytes 147480
  2.2 0.0 copy-start.1
  2.2 0.9 %copy-done.1 = bf16[288,256]{1,0:T(8,128)(2,1)S(1)} copy-done((bf16[288,256]{1,0:T(8,128)(2,1)S(1)}, bf16[288,256]{1,0:T(8,128)(2,1)}, u32[]{:S(2)}) %copy-start.1) | copy-done | bytes 147480
  3.1 0.0 copy-start.2
  3.1 0.8 copy-done.2
  3.9 76.0 %shard_map.84 = (f32[288,256]{1,0:T(8,128)S(1)}, f32[288,256]{1,0:T(8,128)S(1)}, f32[96,256]{1,0:T(8,128)S(1)}) custom-call(bf16[288,256]{1,0:T(8,128)(2,1)S(1)} %copy-done, bf16[288,256]{1,0:T(8,128)(2,1)S(1)} %copy-done.1, bf16[64,256]{1,0:T(8,128)(2,1)S(1)} %copy-done.2, f32[1,256]{1,0:T(1,128)S(1)} %bitcast.2), custom_call_target="tpu_custom_call" | custom-call | tf_op jit(solution)/shard_map/pallas_call | solution.py:456
  79.9 0.0 copy-start.4
  79.9 0.6 copy-done.4
  80.5 1.7 %shard_map.85 = (f32[96,192]{1,0:T(8,128)}, f32[96,192]{1,0:T(8,128)}, bf16[288,256]{1,0:T(8,128)(2,1)}, f32[288,256]{1,0:T(8,128)}) custom-call(f32[288,256]{1,0:T(8,128)S(1)} %get-tuple-element.7.total, f32[288,256]{1,0:T(8,128)S(1)} %get-tuple-element.8.scaled, f32[96,256]{1,0:T(8,128)S(1)} %get-tuple-element.9.inner, f32[1,256]{1,0:T(1,128)S(1)} %bitcast.3, ...), custom_call_target="tpu_custom_call" | custom-call | tf_op jit(solution)/shard_map/pallas_call | solution.py:498
Async XLA Ops:
  0.6 0.7 copy-start.3
  1.3 0.9 %copy-start = (bf16[288,256]{1,0:T(8,128)(2,1)S(1)}, bf16[288,256]{1,0:T(8,128)(2,1)}, u32[]{:S(2)}) copy-start(bf16[288,256]{1,0:T(8,128)(2,1)} %attn_hbm.1) | copy-start | bytes 442372
  2.2 0.9 %copy-start.1 = (bf16[288,256]{1,0:T(8,128)(2,1)S(1)}, bf16[288,256]{1,0:T(8,128)(2,1)}, u32[]{:S(2)}) copy-start(bf16[288,256]{1,0:T(8,128)(2,1)} %resid_hbm.1) | copy-start | bytes 442372
  3.1 0.8 copy-start.2
  79.9 0.7 copy-start.4
